TPU v7x, 128 devices: a whole 4x4x4 slice. The times are simulated.
128 devices in a mesh: dp: 8 (over z_hi, x), expert: 16 (over z_lo, y, core).
Axes of the slice: x: 4, y: 4, z: 4 (z_hi: 2, z_lo: 2; z = z_hi * 2 + z_lo), core: 2. Of those that a mesh axis runs over, the one named last changes fastest.
Arguments:
- frames: bfloat16 [8, 2048, 1536], P('dp', 'expert'), may hold values from -6 to 6
- lengths: int32 [8], P('dp'), may hold values from 1024 to 2048, as said below
- kernel: float32 [31, 1536], replicated, may hold values from -1 to 1
- expert_ids: int32 [8, 2048, 2], P('dp', 'expert'), may hold values from 0 to 15, all different within a row; in each aligned block of 128 rows (0 to 127, 128 to 255, ..., all dimensions but the last counted through in order) at most 18 rows name the same one
- gate_weights: float32 [8, 2048, 2], P('dp', 'expert'), may hold values from 0.1 to 0.9
- w_in: bfloat16 [16, 1536, 6144], P('expert', None, 'dp'), may hold values from -0.15625 to 0.15625
- w_out: bfloat16 [16, 6144, 1536], P('expert', 'dp'), may hold values from -0.078125 to 0.078125
- cotangent: bfloat16 [8, 2048, 1536], P('dp', 'expert'), may hold values from -6 to 6
Outputs:
- grad_frames: bfloat16 [8, 2048, 1536], P('dp', 'expert')
- grad_kernel: float32 [31, 1536], P(None, ('dp', 'expert'))
- grad_w_in: float32 [16, 1536, 6144], P('expert', None, 'dp')
- grad_w_out: float32 [16, 6144, 1536], P('expert', 'dp')
Inputs may be any that keep to these rules, and one draw needn't show every extreme that they name: `lengths`: valid frames of each utterance; at least one utterance has all 2048. `expert_ids`: each frame names two different experts; among the 128 frames of one index of expert in one utterance no expert is named more than 18 times, a bound that some block reaches.
All inputs are finite; a program needn't handle non-finite values.
Results may differ from a plain program's by a relative error of at most 0.006.
Values may be sent and summed in bfloat16 or wider, within the bound.
No kernel may reach another device: no remote copies, remote signals or barrier semaphores. Data moves between devices by JAX's collectives and lax.ppermute only.
A program may use at most 192 MiB of HBM per device.

v0:
```python
import jax
import jax.numpy as jnp
from jax import lax
from jax.experimental import pallas as pl
from jax.experimental.pallas import tpu as pltpu
from jax.sharding import PartitionSpec as P

EPSILON = 1e-06
AXES = ("dp", "expert")
SLOTS = 18
X, Y, Z = 4, 4, 4


def number_of(x, y, z, core):
    return ((z // 2) * X + x) * 16 + (z % 2) * 8 + y * 2 + core


def moved(rows, dx=0, dy=0, dz=0, dc=0):
    pairs = []
    for x in range(X):
        for y in range(Y):
            for z in range(Z):
                for core in range(2):
                    pairs.append(
                        (
                            number_of(x, y, z, core),
                            number_of((x + dx) % X, (y + dy) % Y, (z + dz) % Z, core ^ dc),
                        )
                    )
    return lax.ppermute(rows, AXES, pairs)


def extended(cells, width):
    count = lax.axis_size("expert")
    ends = count - 1
    head = cells[:width]
    tail = cells[-width:]
    return jnp.concatenate(
        [
            lax.ppermute(tail, "expert", [(i, i + 1) for i in range(ends)]),
            cells,
            lax.ppermute(head, "expert", [(i + 1, i) for i in range(ends)]),
        ],
        axis=0,
    )


def rms_scale(values):
    return values * lax.rsqrt(jnp.mean(values * values, axis=-1, keepdims=True) + EPSILON)


def dot(a, b, ca, cb, kind=jnp.float32):
    return lax.dot_general(
        a, b, (((ca,), (cb,)), ((), ())), preferred_element_type=jnp.float32
    ).astype(kind)


def order():
    place = jnp.arange(16 * SLOTS, dtype=jnp.int32)
    slot = place % SLOTS
    source = (place // SLOTS) % 4
    rz = (place // (4 * SLOTS)) % 2
    rc = place // (8 * SLOTS)
    taken = source * 4 * SLOTS + rz * 2 * SLOTS + rc * SLOTS + slot
    return (taken[:, None] == place[None, :]).astype(jnp.bfloat16)


X_GROUPS = [[0, 1, 2, 3], [4, 5, 6, 7]]


def after(value, *earlier):
    return lax.optimization_barrier((value, *earlier))[0]


def together(*values):
    return lax.optimization_barrier(values)


def along_y(rows):
    part = 4 * SLOTS
    pieces = [rows[part * r : part * r + part] for r in range(4)]
    return pieces[:1] + [moved(pieces[r], dy=r) for r in range(1, 4)]


def to_cores(pieces, arrange):
    part = 4 * SLOTS
    placed = dot(arrange, jnp.concatenate(pieces, axis=0), 1, 0, jnp.bfloat16)
    core = moved(placed[2 * part :], dc=1)
    same = jnp.concatenate([placed[:part], core[:part]], axis=0)
    other = jnp.concatenate([placed[part : 2 * part], core[part:]], axis=0)
    return same, other


def neighbours(same, other):
    return moved(other, dz=1), moved(other, dz=-1), moved(same, dx=1), moved(same, dx=-1)


def gathered(up, down):
    other = jnp.concatenate([up, down], axis=0)
    return lax.all_gather(other, "dp", axis=0, tiled=True, axis_index_groups=X_GROUPS)


def total(*terms):
    out = terms[0].astype(jnp.float32)
    for term in terms[1:]:
        out = out + term.astype(jnp.float32)
    return out.astype(jnp.bfloat16)


def sent_back(first, other, second, arrange, grad_in, grad_out):
    part = 4 * SLOTS
    same = total(
        second[: 2 * part],
        moved(first[: 2 * part], dx=-1),
        moved(first[2 * part :], dx=1),
        moved(second[2 * part :], dx=2),
    )
    other = total(moved(other[: 2 * part], dz=-1), moved(other[2 * part :], dz=1))
    same, other, grad_in, grad_out = together(same, other, grad_in, grad_out)
    core = moved(jnp.concatenate([same[part:], other[part:]], axis=0), dc=1)
    placed = jnp.concatenate([same[:part], other[:part], core], axis=0)
    rows = dot(arrange, placed, 0, 0, jnp.bfloat16)
    pieces = [rows[part * r : part * r + part] for r in range(4)]
    pieces = pieces[:1] + [moved(pieces[r], dy=-r) for r in range(1, 4)]
    return jnp.concatenate(pieces, axis=0), grad_in, grad_out


def tap_sums_kernel(resid_cot, rim, out, wide, sums):
    rows, width = resid_cot.shape
    wide[...] = rim[...].astype(jnp.float32)
    sums[...] = jnp.zeros_like(sums)

    @pl.loop(0, width // 128)
    def _(tile):
        lanes = pl.ds(pl.multiple_of(tile * 128, 128), 128)
        cot = resid_cot[:, lanes]
        for tap in range(31):
            product = cot * wide[pl.ds(tap, rows), lanes]
            sums[pl.ds(tap, 1), lanes] = jnp.sum(product, axis=0, keepdims=True)

    share = width // 8
    for part in range(8):
        low = part * share // 128 * 128
        high = min(low + 384, width)
        piece = sums[:, low:high]
        shift = part * share - low
        if shift:
            piece = pltpu.roll(piece, high - low - shift, 1)
        out[part] = piece[:, :256]


def tap_sums(resid_cot, rim):
    width = resid_cot.shape[1]
    return pl.pallas_call(
        tap_sums_kernel,
        out_shape=jax.ShapeDtypeStruct((8, 32, 256), jnp.float32),
        scratch_shapes=[
            pltpu.VMEM(rim.shape, jnp.float32),
            pltpu.VMEM((32, width), jnp.float32),
        ],
        compiler_params=pltpu.CompilerParams(vmem_limit_bytes=16 * 2**20),
        name="tap_sums",
    )(resid_cot, rim)


def split_columns_kernel(share, parts, out):
    whole = parts[0]
    for part in range(1, 8):
        whole = whole + parts[part]
    whole = jnp.concatenate([whole, jnp.zeros((32, 128), jnp.float32)], axis=1)
    for part in range(16):
        piece = pltpu.roll(whole, 384 - share * part, 1) if part else whole
        out[part] = piece[:, :128]


def split_columns(parts, share):
    return pl.pallas_call(
        lambda *refs: split_columns_kernel(share, *refs),
        out_shape=jax.ShapeDtypeStruct((16, 32, 128), jnp.float32),
        compiler_params=pltpu.CompilerParams(vmem_limit_bytes=16 * 2**20),
        name="split_columns",
    )(parts)


def local(frames, lengths, kernel, expert_ids, gate_weights, w_in, w_out, cotangent):
    block_len = frames.shape[1]
    model_width = frames.shape[2]
    tap_count = kernel.shape[0]
    half_width = tap_count // 2
    place = lax.axis_index("expert")
    my_z, my_y, my_core = place // 8, (place // 2) % 4, place % 2
    positions = place * block_len + jnp.arange(block_len, dtype=jnp.int32)
    frame_mask = (positions < lengths[0]).astype(jnp.float32)
    arrange = order()

    ids = expert_ids[0]
    experts = jnp.arange(16, dtype=jnp.int32)
    named = (ids[:, :, None] == experts).astype(jnp.float32)
    both = named[:, 0] + named[:, 1]
    earlier = jnp.cumsum(both, axis=0) - both
    base = (
        ((experts // 2 - my_y) % 4) * 72
        + (experts // 8 != my_z) * 36
        + (experts % 2 != my_core) * 18
    ).astype(jnp.float32)
    target = jnp.sum(named * (earlier + base)[:, None, :], axis=2).astype(jnp.int32)
    rows = jnp.arange(16 * SLOTS, dtype=jnp.int32)
    hit = rows[:, None, None] == target[None]
    frame_place = jnp.any(hit, axis=2).astype(jnp.bfloat16)
    coeff = 0.5 * gate_weights[0] * frame_mask[:, None]
    row_coeff = jnp.sum(jnp.where(hit, coeff[None], 0.0), axis=(1, 2))

    cot_rows = (row_coeff[:, None] * dot(frame_place, cotangent[0], 1, 0)).astype(jnp.bfloat16)
    masked = (frames[0].astype(jnp.float32) * frame_mask[:, None]).astype(jnp.bfloat16)
    frame_rim = extended(masked, half_width)
    rim = jnp.concatenate([frame_rim, jnp.zeros((2, model_width), jnp.bfloat16)], axis=0)
    conv = jnp.zeros((block_len, model_width), jnp.float32)
    for tap in range(tap_count):
        conv = conv + kernel[tap] * frame_rim[tap : tap + block_len].astype(jnp.float32)
    resid = frames[0].astype(jnp.float32) + conv
    normed_exact, norm_back = jax.vjp(rms_scale, resid)
    normed = normed_exact.astype(jnp.bfloat16)
    normed_rows = dot(frame_place, normed, 1, 0, jnp.bfloat16)

    y_cot = along_y(cot_rows)
    *y_cot, normed_rows = together(*y_cot, normed_rows)
    same_cot, other_cot = to_cores(y_cot, arrange)
    up, down, s1, s3, same_cot, normed_rows = together(
        *neighbours(same_cot, other_cot), same_cot, normed_rows
    )
    gathered_cot = gathered(up, down)
    first_cot = jnp.concatenate([s1, s3], axis=0)
    weight_in = w_in[0]
    weight_out = w_out[0]
    s2, first_far, same_cot, *y_normed = together(
        moved(s1, dx=1), moved(first_cot, dz=2), same_cot, *along_y(normed_rows)
    )
    same, other = to_cores(y_normed, arrange)
    second_cot = jnp.concatenate([same_cot, s2], axis=0)
    first_cot = jnp.concatenate([first_cot, first_far], axis=0)
    first_hidden_cot = dot(first_cot, weight_out, 1, 1)
    up, down, s1, s3 = neighbours(same, other)
    up, down, second_cot, first_hidden_cot = together(up, down, second_cot, first_hidden_cot)
    other_normed = gathered(up, down)
    second_far, s1, s3, same = together(moved(second_cot, dz=2), s1, s3, same)
    gathered_hidden_cot = dot(gathered_cot, weight_out, 1, 1)
    second_cot = jnp.concatenate([second_cot, second_far], axis=0)
    second_hidden_cot = dot(second_cot, weight_out, 1, 1)
    far1, far3, s2, same, second_hidden_cot, gathered_hidden_cot = together(
        moved(s1, dz=2),
        moved(s3, dz=2),
        moved(s3, dx=-1),
        same,
        second_hidden_cot,
        gathered_hidden_cot,
    )
    first_normed = jnp.concatenate([s1, s3, far1, far3], axis=0)
    far, far2 = moved(same, dz=2), moved(s2, dz=2)

    def expert(rows_normed, hidden_cot):
        pre_act = dot(rows_normed, weight_in, 1, 0)
        sigmoid_pre = jax.nn.sigmoid(pre_act)
        hidden = (pre_act * sigmoid_pre).astype(jnp.bfloat16)
        pre_cot = (hidden_cot * sigmoid_pre * (1.0 + pre_act * (1.0 - sigmoid_pre))).astype(
            jnp.bfloat16
        )
        return hidden, pre_cot, dot(pre_cot, weight_in, 1, 1, jnp.bfloat16)

    half = 8 * SLOTS * 2
    other_hidden, other_pre_cot, other_part = expert(other_normed, gathered_hidden_cot)
    first_normed, far, far2, _ = together(first_normed, far, far2, other_part)
    first_hidden, first_pre_cot, first_part = expert(first_normed, first_hidden_cot)
    first_back = moved(first_part[half:], dz=2)
    second_normed = jnp.concatenate([same, s2, far, far2], axis=0)
    second_normed = after(second_normed, first_part)
    second_hidden, second_pre_cot, second_part = expert(second_normed, second_hidden_cot)
    first_back = after(first_back, second_part)
    first_sum = total(first_part[:half], first_back)
    second_sum = total(second_part[:half], moved(second_part[half:], dz=2))

    other_hidden, other_pre_cot, second_part = together(other_hidden, other_pre_cot, second_part)
    grad_out = dot(other_hidden, gathered_cot, 0, 0)
    grad_in = dot(other_normed, other_pre_cot, 0, 0)
    first_hidden, second_hidden, first_cot, second_part = together(
        first_hidden, second_hidden, first_cot, second_part
    )
    cots = jnp.concatenate([first_cot, second_cot], axis=0)
    hiddens = jnp.concatenate([first_hidden, second_hidden], axis=0)
    grad_out = grad_out + dot(hiddens, cots, 0, 0)
    other_part = lax.psum_scatter(
        other_part, "dp", scatter_dimension=0, tiled=True, axis_index_groups=X_GROUPS
    )
    first_pre_cot, second_pre_cot, first_normed, first_sum = together(
        first_pre_cot, second_pre_cot, first_normed, first_sum
    )
    pre_cots = jnp.concatenate([first_pre_cot, second_pre_cot], axis=0)
    normeds = jnp.concatenate([first_normed, second_normed], axis=0)
    grad_in = grad_in + dot(normeds, pre_cots, 0, 0)
    returned, grad_in, grad_out = sent_back(
        first_sum, other_part, second_sum, arrange, grad_in, grad_out
    )
    normed_cot = dot(frame_place, returned, 0, 0)

    resid_cot = cotangent[0].astype(jnp.float32) + norm_back(normed_cot)[0]
    taps = tap_sums(resid_cot, rim)
    taps = split_columns(lax.all_to_all(taps, "dp", 0, 0, tiled=True), model_width // 128)
    taps = lax.all_to_all(taps, "expert", 0, 0, tiled=True)
    grad_kernel = taps[:, :tap_count, : model_width // 128].sum(axis=0)
    grad_rim = extended(resid_cot, half_width)
    spread_back = jnp.zeros((block_len, model_width), jnp.float32)
    for tap in range(tap_count):
        offset = 2 * half_width - tap
        spread_back = spread_back + kernel[tap] * grad_rim[offset : offset + block_len]
    grad_frames = (resid_cot + frame_mask[:, None] * spread_back).astype(jnp.bfloat16)
    return (grad_frames[None], grad_kernel, grad_in[None], grad_out[None])


def solution(mesh):
    return jax.shard_map(
        local,
        mesh=mesh,
        in_specs=(
            P("dp", "expert", None),
            P("dp"),
            P(),
            P("dp", "expert", None),
            P("dp", "expert", None),
            P("expert", None, "dp"),
            P("expert", "dp", None),
            P("dp", "expert", None),
        ),
        out_specs=(
            P("dp", "expert", None),
            P(None, ("dp", "expert")),
            P("expert", None, "dp"),
            P("expert", "dp", None),
        ),
        check_vma=False,
    )
```

profile of v0, /device:TPU:1, one launch (start us, length us, event | category | flops | bytes accessed | tf_op | source)
XLA Modules:
  0.0 310.7 jit_solution(7138831835357205674)
XLA Ops:
  9.8 4.6 %collective-permute-start.3 = (bf16[15,1536]{1,0:T(8,128)(2,1)}, bf16[15,1536]{1,0:T(8,128)(2,1)S(1)}, u32[]{:S(2)}, u32[]{:S(2)}) collective-permute-start(bf16[15,1536]{1,0:T(8,128)(2,1)} %get-tuple-element.189), channel_id=1, source_target_pairs={{0,1},{1,2},{2,3},{3,4},{4,5},{5,6},{6,7},{7,8},{8,9},{9,10},{10,1... | collective-permute-start | bytes 138248 | tf_op jit(solution)/shard_map/ppermute | solution.py:40
  25.1 6.3 %multiply_reduce_fusion.1 = (f32[128]{0:T(128)S(1)}, f32[128,1536]{1,0:T(8,128)S(1)}) fusion(bf16[15,1536]{1,0:T(8,128)(2,1)} %copy-done.22, bf16[128,1536]{1,0:T(8,128)(2,1)S(1)} %fusion.149, f32[1536]{0:T(1024)S(1)} %get-tuple-element.149, f32[1536]{0:T(1024)S(1)} %get-tuple-element.150, f32[1536]{0:T(1024)S(1)} %get-tuple-element.121, ...), kind=kLoop, calls=%fused_computation.273 | loop fusion | flops 36568960 | bytes 1856000 | tf_op jit(solution)/shard_map/jvp()/reduce_sum | solution.py:49
  43.6 6.6 %collective-permute-done.7 = bf16[144,1536]{1,0:T(8,128)(2,1)S(1)} collective-permute-done((bf16[144,1536]{1,0:T(8,128)(2,1)S(1)}, bf16[144,1536]{1,0:T(8,128)(2,1)S(1)}, u32[]{:S(2)}, u32[]{:S(2)}) %collective-permute-start.7) | collective-permute-done | bytes 442400 | tf_op jit(solution)/shard_map/ppermute | solution.py:30
  50.2 3.2 %collective-permute-done.6 = bf16[144,1536]{1,0:T(8,128)(2,1)S(1)} collective-permute-done((bf16[144,1536]{1,0:T(8,128)(2,1)S(1)}, bf16[144,1536]{1,0:T(8,128)(2,1)S(1)}, u32[]{:S(2)}, u32[]{:S(2)}) %collective-permute-start.6) | collective-permute-done | bytes 442400 | tf_op jit(solution)/shard_map/ppermute | solution.py:30
  67.9 5.6 %collective-permute-done.12 = bf16[72,1536]{1,0:T(8,128)(2,1)S(1)} collective-permute-done((bf16[72,1536]{1,0:T(8,128)(2,1)S(1)}, bf16[72,1536]{1,0:T(8,128)(2,1)S(1)}, u32[]{:S(2)}, u32[]{:S(2)}) %collective-permute-start.12) | collective-permute-done | bytes 221216 | tf_op jit(solution)/shard_map/ppermute | solution.py:30
  73.5 5.4 %collective-permute-done.11 = bf16[288,1536]{1,0:T(8,128)(2,1)S(1)} collective-permute-done((bf16[288,1536]{1,0:T(8,128)(2,1)S(1)}, bf16[288,1536]{1,0:T(8,128)(2,1)S(1)}, u32[]{:S(2)}, u32[]{:S(2)}) %collective-permute-start.11) | collective-permute-done | bytes 884768 | tf_op jit(solution)/shard_map/ppermute | solution.py:30
  87.5 11.7 %collective-permute-start.16 = (bf16[144,1536]{1,0:T(8,128)(2,1)S(1)}, bf16[144,1536]{1,0:T(8,128)(2,1)S(1)}, u32[]{:S(2)}, u32[]{:S(2)}) collective-permute-start(bf16[144,1536]{1,0:T(8,128)(2,1)S(1)} %pad_maximum_fusion.10), channel_id=1, source_target_pairs={{0,8},{1,9},{8,64},{9,65},{64,72},{65,73},{72,0},{73,1},{2,10},{3,... | collective-permute-start | bytes 1327112 | tf_op jit(solution)/shard_map/ppermute | solution.py:30
  102.0 9.6 %collective-permute-done.16 = bf16[144,1536]{1,0:T(8,128)(2,1)S(1)} collective-permute-done((bf16[144,1536]{1,0:T(8,128)(2,1)S(1)}, bf16[144,1536]{1,0:T(8,128)(2,1)S(1)}, u32[]{:S(2)}, u32[]{:S(2)}) %collective-permute-start.16) | collective-permute-done | bytes 442400 | tf_op jit(solution)/shard_map/ppermute | solution.py:30
  117.3 9.9 %collective-permute-done.20 = bf16[144,1536]{1,0:T(8,128)(2,1)} collective-permute-done((bf16[144,1536]{1,0:T(8,128)(2,1)}, bf16[144,1536]{1,0:T(8,128)(2,1)}, u32[]{:S(2)}, u32[]{:S(2)}) %collective-permute-start.20) | collective-permute-done | bytes 442400 | tf_op jit(solution)/shard_map/ppermute | solution.py:30
  127.1 3.4 %collective-permute-done.19 = bf16[144,1536]{1,0:T(8,128)(2,1)} collective-permute-done((bf16[144,1536]{1,0:T(8,128)(2,1)}, bf16[144,1536]{1,0:T(8,128)(2,1)}, u32[]{:S(2)}, u32[]{:S(2)}) %collective-permute-start.19) | collective-permute-done | bytes 442400 | tf_op jit(solution)/shard_map/ppermute | solution.py:30
  130.5 3.8 %collective-permute-done.18 = bf16[288,1536]{1,0:T(8,128)(2,1)S(1)} collective-permute-done((bf16[288,1536]{1,0:T(8,128)(2,1)}, bf16[288,1536]{1,0:T(8,128)(2,1)S(1)}, u32[]{:S(2)}, u32[]{:S(2)}) %collective-permute-start.18) | collective-permute-done | bytes 884768 | tf_op jit(solution)/shard_map/ppermute | solution.py:30
  139.9 4.7 %fusion.20 = f32[576,768]{1,0:T(8,128)} fusion(bf16[1,768,1536]{2,1,0:T(8,128)(2,1)} %param.14, bf16[288,1536]{1,0:T(8,128)(2,1)S(1)} %collective-permute-done.18, bf16[288,1536]{1,0:T(8,128)(2,1)} %get-tuple-element.70), kind=kOutput, calls=%fused_computation.61 | convolution fusion | flops 1362493440 | bytes 5898240 | tf_op jit(solution)/shard_map/dot_general | solution.py:53
  144.6 7.5 %fusion.18 = f32[1152,768]{1,0:T(8,128)} fusion(bf16[1152,1536]{1,0:T(8,128)(2,1)} %all-gather.3.cloned.1.call-done, bf16[1,768,1536]{2,1,0:T(8,128)(2,1)} %param.14), kind=kOutput, calls=%fused_computation.59 | convolution fusion | flops 2717908992 | bytes 9437184 | tf_op jit(solution)/shard_map/dot_general | solution.py:53
  152.1 5.2 %collective-permute-done.21 = bf16[144,1536]{1,0:T(8,128)(2,1)} collective-permute-done((bf16[144,1536]{1,0:T(8,128)(2,1)}, bf16[144,1536]{1,0:T(8,128)(2,1)}, u32[]{:S(2)}, u32[]{:S(2)}) %collective-permute-start.21) | collective-permute-done | bytes 442400 | tf_op jit(solution)/shard_map/ppermute | solution.py:30
  165.5 5.1 %fusion.16 = f32[1152,768]{1,0:T(8,128)S(1)} fusion(bf16[1152,1536]{1,0:T(8,128)(2,1)} %all-gather.5.cloned.1.call-done, bf16[1,1536,768]{2,1,0:T(8,128)(2,1)S(1)} %copy-done), kind=kOutput, calls=%fused_computation.57 | convolution fusion | flops 2717908992 | bytes 9437184 | tf_op jit(solution)/shard_map/dot_general | solution.py:53
  174.4 4.5 %convolution_convert_fusion = bf16[1152,1536]{1,0:T(8,128)(2,1)} fusion(bf16[1152,768]{1,0:T(8,128)(2,1)S(1)} %get-tuple-element.92, bf16[1,1536,768]{2,1,0:T(8,128)(2,1)S(1)} %copy-done), kind=kOutput, calls=%fused_computation | convolution fusion | flops 2719678464 | bytes 7667712 | tf_op jit(solution)/shard_map/dot_general | solution.py:53
  178.9 4.0 %multiply_convert_fusion.3 = (bf16[576,768]{1,0:T(8,128)(2,1)S(1)}, bf16[576,768]{1,0:T(8,128)(2,1)S(1)}) fusion(f32[576,768]{1,0:T(8,128)} %fusion.22, bf16[576,1536]{1,0:T(8,128)(2,1)} %pad_maximum_fusion, bf16[1,1536,768]{2,1,0:T(8,128)(2,1)S(1)} %copy-done), kind=kOutput, calls=%fused_computation.105 | convolution fusion | flops 1363820544 | bytes 7667712 | tf_op jit(solution)/shard_map/dot_general | solution.py:53
  194.7 3.4 %fusion.235 = f32[1536,768]{1,0:T(8,128)S(1)} fusion(bf16[1152,1536]{1,0:T(8,128)(2,1)S(1)} %copy-done.70, bf16[1152,768]{1,0:T(8,128)(2,1)S(1)} %copy-done.13), kind=kOutput, calls=%fused_computation.461 | convolution fusion | flops 2717908992 | bytes 10027008 | tf_op jit(solution)/shard_map/dot_general | solution.py:53
  198.1 3.3 %fusion.236 = f32[768,1536]{1,0:T(8,128)S(1)} fusion(bf16[1152,768]{1,0:T(8,128)(2,1)S(1)} %copy-done.11, bf16[1152,1536]{1,0:T(8,128)(2,1)S(1)} %copy-done.69), kind=kOutput, calls=%fused_computation.462 | convolution fusion | flops 2717908992 | bytes 10027008 | tf_op jit(solution)/shard_map/dot_general | solution.py:53
  201.4 5.6 %convolution_add_fusion = f32[768,1536]{1,0:T(8,128)} fusion(f32[768,1536]{1,0:T(8,128)S(1)} %fusion.236, bf16[288,1536]{1,0:T(8,128)(2,1)S(1)} %copy-done.73, bf16[288,1536]{1,0:T(8,128)(2,1)S(1)} %copy-done.17, bf16[576,1536]{1,0:T(8,128)(2,1)S(1)} %copy-done.26, bf16[576,768]{1,0:T(8,128)(2,1)S(1)} %get-tuple-element.98, ...), kind=kOutput, calls=%fused_computation.29 | convolution fusion | flops 2733244416 | bytes 14745600 | tf_op jit(solution)/shard_map/dot_general | solution.py:53
  209.0 4.3 %collective-permute-start.28 = (bf16[144,1536]{1,0:T(8,128)(2,1)}, bf16[144,1536]{1,0:T(8,128)(2,1)}, u32[]{:S(2)}, u32[]{:S(2)}) collective-permute-start(bf16[144,1536]{1,0:T(8,128)(2,1)} %get-tuple-element.165), channel_id=1, source_target_pairs={{0,48},{1,49},{8,56},{9,57},{64,112},{65,113},{72,120},{73,121},{2... | collective-permute-start | bytes 1327112 | tf_op jit(solution)/shard_map/ppermute | solution.py:30
  213.3 13.4 %collective-permute-done.26 = bf16[288,1536]{1,0:T(8,128)(2,1)S(1)} collective-permute-done((bf16[288,1536]{1,0:T(8,128)(2,1)S(1)}, bf16[288,1536]{1,0:T(8,128)(2,1)S(1)}, u32[]{:S(2)}, u32[]{:S(2)}) %collective-permute-start.26) | collective-permute-done | bytes 884768 | tf_op jit(solution)/shard_map/ppermute | solution.py:30
  231.5 5.1 %convolution_add_fusion.1 = f32[1536,768]{1,0:T(8,128)} fusion(f32[1536,768]{1,0:T(8,128)S(1)} %fusion.235, bf16[576,1536]{1,0:T(8,128)(2,1)S(1)} %pad_maximum_fusion.1, bf16[576,1536]{1,0:T(8,128)(2,1)S(1)} %copy-done.7, bf16[576,768]{1,0:T(8,128)(2,1)S(1)} %get-tuple-element.95, bf16[576,768]{1,0:T(8,128)(2,1)S(1)} %get-tuple-element.94), kind=kOutput, calls=%fused_computation.30 | convolution fusion | flops 2729705472 | bytes 14745600 | tf_op jit(solution)/shard_map/dot_general | solution.py:53
  241.8 6.1 %collective-permute-done.31 = bf16[144,1536]{1,0:T(8,128)(2,1)S(1)} collective-permute-done((bf16[144,1536]{1,0:T(8,128)(2,1)S(1)}, bf16[144,1536]{1,0:T(8,128)(2,1)S(1)}, u32[]{:S(2)}, u32[]{:S(2)}) %collective-permute-start.31) | collective-permute-done | bytes 442400 | tf_op jit(solution)/shard_map/ppermute | solution.py:30
  250.4 3.2 %collective-permute-start.33 = (bf16[144,1536]{1,0:T(8,128)(2,1)S(1)}, bf16[144,1536]{1,0:T(8,128)(2,1)S(1)}, u32[]{:S(2)}, u32[]{:S(2)}) collective-permute-start(bf16[144,1536]{1,0:T(8,128)(2,1)S(1)} %pad_maximum_fusion.12), channel_id=1, source_target_pairs={{0,1},{1,0},{8,9},{9,8},{64,65},{65,64},{72,73},{73,72},{2,3},{3,2... | collective-permute-start | bytes 1327112 | tf_op jit(solution)/shard_map/ppermute | solution.py:30
  263.8 5.7 %collective-permute-done.35 = bf16[72,1536]{1,0:T(8,128)(2,1)S(1)} collective-permute-done((bf16[72,1536]{1,0:T(8,128)(2,1)S(1)}, bf16[72,1536]{1,0:T(8,128)(2,1)S(1)}, u32[]{:S(2)}, u32[]{:S(2)}) %collective-permute-start.35) | collective-permute-done | bytes 221216 | tf_op jit(solution)/shard_map/ppermute | solution.py:30
  271.9 3.7 %tap_sums.1 = f32[8,32,256]{2,1,0:T(8,128)S(1)} custom-call(f32[128,1536]{1,0:T(8,128)S(1)} %fusion.150.resid_cot, bf16[160,1536]{1,0:T(8,128)(2,1)S(1)} %maximum_maximum_fusion.rim), custom_call_target="tpu_custom_call" | custom-call | tf_op jit(solution)/shard_map/tap_sums/pallas_call | solution.py:154
  276.3 3.5 %all-to-all-start = ((f32[8,32,256]{2,1,0:T(8,128)}), f32[8,32,256]{2,1,0:T(8,128)S(1)}, u32[]{:S(2)}, u32[]{:S(2)}) async-start(f32[8,32,256]{2,1,0:T(8,128)} %copy-done.1), calls=%async_computation.1 | async-start | bytes 524288 | tf_op jit(solution)/shard_map/all_to_all | solution.py:306
  280.6 3.1 %collective-permute-start.37 = (f32[15,1536]{1,0:T(8,128)}, f32[15,1536]{1,0:T(8,128)S(1)}, u32[]{:S(2)}, u32[]{:S(2)}) collective-permute-start(f32[15,1536]{1,0:T(8,128)} %get-tuple-element.179), channel_id=1, source_target_pairs={{1,0},{2,1},{3,2},{4,3},{5,4},{6,5},{7,6},{8,7},{9,8},{10,9},{11,1... | collective-permute-start | bytes 276488 | tf_op jit(solution)/shard_map/ppermute | solution.py:42
  283.7 3.1 %collective-permute-start.38 = (f32[15,1536]{1,0:T(8,128)}, f32[15,1536]{1,0:T(8,128)}, u32[]{:S(2)}, u32[]{:S(2)}) collective-permute-start(f32[15,1536]{1,0:T(8,128)} %get-tuple-element.180), channel_id=1, source_target_pairs={{0,1},{1,2},{2,3},{3,4},{4,5},{5,6},{6,7},{7,8},{8,9},{9,10},{10,1... | collective-permute-start | bytes 276488 | tf_op jit(solution)/shard_map/ppermute | solution.py:40
  288.7 7.4 %all-to-all-start.1 = ((f32[16,32,128]{2,1,0:T(8,128)}), f32[16,32,128]{2,1,0:T(8,128)S(1)}, u32[]{:S(2)}, u32[]{:S(2)}) async-start(f32[16,32,128]{2,1,0:T(8,128)} %split_columns.1), calls=%async_computation.2 | async-start | bytes 524288 | tf_op jit(solution)/shard_map/all_to_all | solution.py:307
  296.2 6.2 %fusion.183 = bf16[1,128,1536]{2,1,0:T(8,128)(2,1)} fusion(f32[128,1536]{1,0:T(8,128)S(1)} %fusion.150.resid_cot, f32[15,1536]{1,0:T(8,128)} %collective-permute-done.38, f32[1536]{0:T(1024)} %copy-done.58, f32[1536]{0:T(1024)} %copy-done.59, f32[1536]{0:T(1024)S(1)} %get-tuple-element.121, f32[1536]{0:T(1024)S(1)} %copy-done.28, f32[1536]{0:T(1024)S(1)} %copy-done.30, ...), kind=kLoop, calls=%fused_computation.333 | loop fusion | flops 18481152 | bytes 1554944 | tf_op jit(solution)/shard_map/broadcast_in_dim | solution.py:315
  (291 shorter events, 116.3 us)
Async XLA Ops:
  7.2 137.4 %all-gather.3.cloned.1.call-start = ((), (), s32[]{:S(2)}) async-start(), calls=%async_computation.3 | async-start | bytes 4423680 | tf_op jit(solution)/shard_map/all_gather | solution.py:100
  9.8 14.6 %collective-permute-start.3 = (bf16[15,1536]{1,0:T(8,128)(2,1)}, bf16[15,1536]{1,0:T(8,128)(2,1)S(1)}, u32[]{:S(2)}, u32[]{:S(2)}) collective-permute-start(bf16[15,1536]{1,0:T(8,128)(2,1)} %get-tuple-element.189), channel_id=1, source_target_pairs={{0,1},{1,2},{2,3},{3,4},{4,5},{5,6},{6,7},{7,8},{8,9},{9,10},{10,1... | collective-permute-start | bytes 138248 | tf_op jit(solution)/shard_map/ppermute | solution.py:40
  18.8 14.2 %collective-permute-start.2 = (bf16[72,1536]{1,0:T(8,128)(2,1)S(1)}, bf16[72,1536]{1,0:T(8,128)(2,1)S(1)}, u32[]{:S(2)}, u32[]{:S(2)}) collective-permute-start(bf16[72,1536]{1,0:T(8,128)(2,1)S(1)} %get-tuple-element.175), channel_id=1, source_target_pairs={{0,6},{1,7},{8,14},{9,15},{64,70},{65,71},{72,78},{73,79},{2,0},{3... | collective-permute-start | bytes 663560 | tf_op jit(solution)/shard_map/ppermute | solution.py:30
  21.9 13.2 %collective-permute-start = (bf16[72,1536]{1,0:T(8,128)(2,1)S(1)}, bf16[72,1536]{1,0:T(8,128)(2,1)S(1)}, u32[]{:S(2)}, u32[]{:S(2)}) collective-permute-start(bf16[72,1536]{1,0:T(8,128)(2,1)S(1)} %get-tuple-element.177), channel_id=1, source_target_pairs={{0,2},{1,3},{8,10},{9,11},{64,66},{65,67},{72,74},{73,75},{2,4},{3... | collective-permute-start | bytes 663560 | tf_op jit(solution)/shard_map/ppermute | solution.py:30
  38.1 12.1 %collective-permute-start.7 = (bf16[144,1536]{1,0:T(8,128)(2,1)S(1)}, bf16[144,1536]{1,0:T(8,128)(2,1)S(1)}, u32[]{:S(2)}, u32[]{:S(2)}) collective-permute-start(bf16[144,1536]{1,0:T(8,128)(2,1)S(1)} %pad_maximum_fusion.8), channel_id=1, source_target_pairs={{0,72},{1,73},{8,0},{9,1},{64,8},{65,9},{72,64},{73,65},{2,74},{3,... | collective-permute-start | bytes 1327112 | tf_op jit(solution)/shard_map/ppermute | solution.py:30
  41.0 12.4 %collective-permute-start.6 = (bf16[144,1536]{1,0:T(8,128)(2,1)S(1)}, bf16[144,1536]{1,0:T(8,128)(2,1)S(1)}, u32[]{:S(2)}, u32[]{:S(2)}) collective-permute-start(bf16[144,1536]{1,0:T(8,128)(2,1)S(1)} %pad_maximum_fusion.8), channel_id=1, source_target_pairs={{0,8},{1,9},{8,64},{9,65},{64,72},{65,73},{72,0},{73,1},{2,10},{3,... | collective-permute-start | bytes 1327112 | tf_op jit(solution)/shard_map/ppermute | solution.py:30
  41.1 12.3 %collective-permute-start.9 = (bf16[144,1536]{1,0:T(8,128)(2,1)S(1)}, bf16[144,1536]{1,0:T(8,128)(2,1)}, u32[]{:S(2)}, u32[]{:S(2)}) collective-permute-start(bf16[144,1536]{1,0:T(8,128)(2,1)S(1)} %pad_maximum_fusion.9), channel_id=1, source_target_pairs={{0,48},{1,49},{8,56},{9,57},{64,112},{65,113},{72,120},{73,121},{2... | collective-permute-start | bytes 1327112 | tf_op jit(solution)/shard_map/ppermute | solution.py:30
  43.6 12.1 %collective-permute-start.8 = (bf16[144,1536]{1,0:T(8,128)(2,1)S(1)}, bf16[144,1536]{1,0:T(8,128)(2,1)}, u32[]{:S(2)}, u32[]{:S(2)}) collective-permute-start(bf16[144,1536]{1,0:T(8,128)(2,1)S(1)} %pad_maximum_fusion.9), channel_id=1, source_target_pairs={{0,16},{1,17},{8,24},{9,25},{64,80},{65,81},{72,88},{73,89},{2,18}... | collective-permute-start | bytes 1327112 | tf_op jit(solution)/shard_map/ppermute | solution.py:30
  56.7 108.8 %all-gather.5.cloned.1.call-start = ((), (), s32[]{:S(2)}) async-start(), calls=%async_computation.4 | async-start | bytes 4423680 | tf_op jit(solution)/shard_map/all_gather | solution.py:100
  56.7 16.8 %collective-permute-start.10 = (bf16[144,1536]{1,0:T(8,128)(2,1)}, bf16[144,1536]{1,0:T(8,128)(2,1)S(1)}, u32[]{:S(2)}, u32[]{:S(2)}) collective-permute-start(bf16[144,1536]{1,0:T(8,128)(2,1)} %collective-permute-done.8), channel_id=1, source_target_pairs={{0,16},{1,17},{8,24},{9,25},{64,80},{65,81},{72,88},{73,89},{2,18}... | collective-permute-start | bytes 1327112 | tf_op jit(solution)/shard_map/ppermute | solution.py:30
  58.1 20.9 %collective-permute-start.11 = (bf16[288,1536]{1,0:T(8,128)(2,1)S(1)}, bf16[288,1536]{1,0:T(8,128)(2,1)S(1)}, u32[]{:S(2)}, u32[]{:S(2)}) collective-permute-start(bf16[288,1536]{1,0:T(8,128)(2,1)S(1)} %pad_maximum_fusion.2), channel_id=1, source_target_pairs={{0,64},{1,65},{8,72},{9,73},{64,0},{65,1},{72,8},{73,9},{2,66},{3,... | collective-permute-start | bytes 2654216 | tf_op jit(solution)/shard_map/ppermute | solution.py:30
  85.0 16.9 %collective-permute-start.17 = (bf16[144,1536]{1,0:T(8,128)(2,1)S(1)}, bf16[144,1536]{1,0:T(8,128)(2,1)S(1)}, u32[]{:S(2)}, u32[]{:S(2)}) collective-permute-start(bf16[144,1536]{1,0:T(8,128)(2,1)S(1)} %pad_maximum_fusion.10), channel_id=1, source_target_pairs={{0,72},{1,73},{8,0},{9,1},{64,8},{65,9},{72,64},{73,65},{2,74},{3,... | collective-permute-start | bytes 1327112 | tf_op jit(solution)/shard_map/ppermute | solution.py:30
  87.5 24.1 %collective-permute-start.16 = (bf16[144,1536]{1,0:T(8,128)(2,1)S(1)}, bf16[144,1536]{1,0:T(8,128)(2,1)S(1)}, u32[]{:S(2)}, u32[]{:S(2)}) collective-permute-start(bf16[144,1536]{1,0:T(8,128)(2,1)S(1)} %pad_maximum_fusion.10), channel_id=1, source_target_pairs={{0,8},{1,9},{8,64},{9,65},{64,72},{65,73},{72,0},{73,1},{2,10},{3,... | collective-permute-start | bytes 1327112 | tf_op jit(solution)/shard_map/ppermute | solution.py:30
  112.6 124.0 %reduce-scatter.2.cloned.1.call-start = ((), (), s32[]{:S(2)}) async-start(), calls=%async_computation.5 | async-start | bytes 4423680 | tf_op jit(solution)/shard_map/reduce_scatter | solution.py:290
  112.7 21.6 %collective-permute-start.18 = (bf16[288,1536]{1,0:T(8,128)(2,1)}, bf16[288,1536]{1,0:T(8,128)(2,1)S(1)}, u32[]{:S(2)}, u32[]{:S(2)}) collective-permute-start(bf16[288,1536]{1,0:T(8,128)(2,1)} %get-tuple-element.70), channel_id=1, source_target_pairs={{0,64},{1,65},{8,72},{9,73},{64,0},{65,1},{72,8},{73,9},{2,66},{3,... | collective-permute-start | bytes 2654216 | tf_op jit(solution)/shard_map/ppermute | solution.py:30
  114.7 12.5 %collective-permute-start.20 = (bf16[144,1536]{1,0:T(8,128)(2,1)}, bf16[144,1536]{1,0:T(8,128)(2,1)}, u32[]{:S(2)}, u32[]{:S(2)}) collective-permute-start(bf16[144,1536]{1,0:T(8,128)(2,1)} %pad_maximum_fusion.11), channel_id=1, source_target_pairs={{0,48},{1,49},{8,56},{9,57},{64,112},{65,113},{72,120},{73,121},{2... | collective-permute-start | bytes 1327112 | tf_op jit(solution)/shard_map/ppermute | solution.py:30
  117.3 13.3 %collective-permute-start.19 = (bf16[144,1536]{1,0:T(8,128)(2,1)}, bf16[144,1536]{1,0:T(8,128)(2,1)}, u32[]{:S(2)}, u32[]{:S(2)}) collective-permute-start(bf16[144,1536]{1,0:T(8,128)(2,1)} %pad_maximum_fusion.11), channel_id=1, source_target_pairs={{0,16},{1,17},{8,24},{9,25},{64,80},{65,81},{72,88},{73,89},{2,18}... | collective-permute-start | bytes 1327112 | tf_op jit(solution)/shard_map/ppermute | solution.py:30
  134.3 23.0 %collective-permute-start.23 = (bf16[144,1536]{1,0:T(8,128)(2,1)}, bf16[144,1536]{1,0:T(8,128)(2,1)}, u32[]{:S(2)}, u32[]{:S(2)}) collective-permute-start(bf16[144,1536]{1,0:T(8,128)(2,1)} %collective-permute-done.20), channel_id=1, source_target_pairs={{0,48},{1,49},{8,56},{9,57},{64,112},{65,113},{72,120},{73,121},{2... | collective-permute-start | bytes 1327112 | tf_op jit(solution)/shard_map/ppermute | solution.py:30
  136.9 20.4 %collective-permute-start.22 = (bf16[144,1536]{1,0:T(8,128)(2,1)}, bf16[144,1536]{1,0:T(8,128)(2,1)}, u32[]{:S(2)}, u32[]{:S(2)}) collective-permute-start(bf16[144,1536]{1,0:T(8,128)(2,1)} %collective-permute-done.20), channel_id=1, source_target_pairs={{0,64},{1,65},{8,72},{9,73},{64,0},{65,1},{72,8},{73,9},{2,66},{3,... | collective-permute-start | bytes 1327112 | tf_op jit(solution)/shard_map/ppermute | solution.py:30
  137.3 20.0 %collective-permute-start.21 = (bf16[144,1536]{1,0:T(8,128)(2,1)}, bf16[144,1536]{1,0:T(8,128)(2,1)}, u32[]{:S(2)}, u32[]{:S(2)}) collective-permute-start(bf16[144,1536]{1,0:T(8,128)(2,1)} %collective-permute-done.19), channel_id=1, source_target_pairs={{0,64},{1,65},{8,72},{9,73},{64,0},{65,1},{72,8},{73,9},{2,66},{3,... | collective-permute-start | bytes 1327112 | tf_op jit(solution)/shard_map/ppermute | solution.py:30
  157.3 21.6 %collective-permute-start.24 = (bf16[144,1536]{1,0:T(8,128)(2,1)}, bf16[144,1536]{1,0:T(8,128)(2,1)}, u32[]{:S(2)}, u32[]{:S(2)}) collective-permute-start(bf16[144,1536]{1,0:T(8,128)(2,1)} %pad_maximum_fusion.11), channel_id=1, source_target_pairs={{0,64},{1,65},{8,72},{9,73},{64,0},{65,1},{72,8},{73,9},{2,66},{3,... | collective-permute-start | bytes 1327112 | tf_op jit(solution)/shard_map/ppermute | solution.py:30
  157.3 21.6 %collective-permute-start.25 = (bf16[144,1536]{1,0:T(8,128)(2,1)}, bf16[144,1536]{1,0:T(8,128)(2,1)}, u32[]{:S(2)}, u32[]{:S(2)}) collective-permute-start(bf16[144,1536]{1,0:T(8,128)(2,1)} %collective-permute-done.23), channel_id=1, source_target_pairs={{0,64},{1,65},{8,72},{9,73},{64,0},{65,1},{72,8},{73,9},{2,66},{3,... | collective-permute-start | bytes 1327112 | tf_op jit(solution)/shard_map/ppermute | solution.py:30
  186.1 21.6 %collective-permute-start.27 = (bf16[288,1536]{1,0:T(8,128)(2,1)S(1)}, bf16[288,1536]{1,0:T(8,128)(2,1)S(1)}, u32[]{:S(2)}, u32[]{:S(2)}) collective-permute-start(bf16[288,1536]{1,0:T(8,128)(2,1)S(1)} %slice.705), channel_id=1, source_target_pairs={{0,64},{1,65},{8,72},{9,73},{64,0},{65,1},{72,8},{73,9},{2,66},{3,... | collective-permute-start | bytes 2654216 | tf_op jit(solution)/shard_map/ppermute | solution.py:30
  193.2 33.5 %collective-permute-start.26 = (bf16[288,1536]{1,0:T(8,128)(2,1)S(1)}, bf16[288,1536]{1,0:T(8,128)(2,1)S(1)}, u32[]{:S(2)}, u32[]{:S(2)}) collective-permute-start(bf16[288,1536]{1,0:T(8,128)(2,1)S(1)} %slice.702), channel_id=1, source_target_pairs={{0,64},{1,65},{8,72},{9,73},{64,0},{65,1},{72,8},{73,9},{2,66},{3,... | collective-permute-start | bytes 2654216 | tf_op jit(solution)/shard_map/ppermute | solution.py:30
  209.0 30.5 %collective-permute-start.28 = (bf16[144,1536]{1,0:T(8,128)(2,1)}, bf16[144,1536]{1,0:T(8,128)(2,1)}, u32[]{:S(2)}, u32[]{:S(2)}) collective-permute-start(bf16[144,1536]{1,0:T(8,128)(2,1)} %get-tuple-element.165), channel_id=1, source_target_pairs={{0,48},{1,49},{8,56},{9,57},{64,112},{65,113},{72,120},{73,121},{2... | collective-permute-start | bytes 1327112 | tf_op jit(solution)/shard_map/ppermute | solution.py:30
  213.3 26.2 %collective-permute-start.29 = (bf16[144,1536]{1,0:T(8,128)(2,1)}, bf16[144,1536]{1,0:T(8,128)(2,1)}, u32[]{:S(2)}, u32[]{:S(2)}) collective-permute-start(bf16[144,1536]{1,0:T(8,128)(2,1)} %get-tuple-element.166), channel_id=1, source_target_pairs={{0,16},{1,17},{8,24},{9,25},{64,80},{65,81},{72,88},{73,89},{2,18}... | collective-permute-start | bytes 1327112 | tf_op jit(solution)/shard_map/ppermute | solution.py:30
  228.7 11.6 %collective-permute-start.30 = (bf16[144,1536]{1,0:T(8,128)(2,1)}, bf16[144,1536]{1,0:T(8,128)(2,1)}, u32[]{:S(2)}, u32[]{:S(2)}) collective-permute-start(bf16[144,1536]{1,0:T(8,128)(2,1)} %slice.706), channel_id=1, source_target_pairs={{0,32},{1,33},{8,40},{9,41},{64,96},{65,97},{72,104},{73,105},{2,3... | collective-permute-start | bytes 1327112 | tf_op jit(solution)/shard_map/ppermute | solution.py:30
  257.1 12.4 %collective-permute-start.35 = (bf16[72,1536]{1,0:T(8,128)(2,1)S(1)}, bf16[72,1536]{1,0:T(8,128)(2,1)S(1)}, u32[]{:S(2)}, u32[]{:S(2)}) collective-permute-start(bf16[72,1536]{1,0:T(8,128)(2,1)S(1)} %get-tuple-element.161), channel_id=1, source_target_pairs={{0,4},{1,5},{8,12},{9,13},{64,68},{65,69},{72,76},{73,77},{2,6},{3... | collective-permute-start | bytes 663560 | tf_op jit(solution)/shard_map/ppermute | solution.py:30
  276.3 11.5 %all-to-all-start = ((f32[8,32,256]{2,1,0:T(8,128)}), f32[8,32,256]{2,1,0:T(8,128)S(1)}, u32[]{:S(2)}, u32[]{:S(2)}) async-start(f32[8,32,256]{2,1,0:T(8,128)} %copy-done.1), calls=%async_computation.1 | async-start | bytes 524288 | tf_op jit(solution)/shard_map/all_to_all | solution.py:306
  280.6 15.6 %collective-permute-start.37 = (f32[15,1536]{1,0:T(8,128)}, f32[15,1536]{1,0:T(8,128)S(1)}, u32[]{:S(2)}, u32[]{:S(2)}) collective-permute-start(f32[15,1536]{1,0:T(8,128)} %get-tuple-element.179), channel_id=1, source_target_pairs={{1,0},{2,1},{3,2},{4,3},{5,4},{6,5},{7,6},{8,7},{9,8},{10,9},{11,1... | collective-permute-start | bytes 276488 | tf_op jit(solution)/shard_map/ppermute | solution.py:42
  283.7 12.4 %collective-permute-start.38 = (f32[15,1536]{1,0:T(8,128)}, f32[15,1536]{1,0:T(8,128)}, u32[]{:S(2)}, u32[]{:S(2)}) collective-permute-start(f32[15,1536]{1,0:T(8,128)} %get-tuple-element.180), channel_id=1, source_target_pairs={{0,1},{1,2},{2,3},{3,4},{4,5},{5,6},{6,7},{7,8},{8,9},{9,10},{10,1... | collective-permute-start | bytes 276488 | tf_op jit(solution)/shard_map/ppermute | solution.py:40
  288.7 14.5 %all-to-all-start.1 = ((f32[16,32,128]{2,1,0:T(8,128)}), f32[16,32,128]{2,1,0:T(8,128)S(1)}, u32[]{:S(2)}, u32[]{:S(2)}) async-start(f32[16,32,128]{2,1,0:T(8,128)} %split_columns.1), calls=%async_computation.2 | async-start | bytes 524288 | tf_op jit(solution)/shard_map/all_to_all | solution.py:307
  (86 other events, 1168.3 us)
Sparse Core Ops, SparseCore 0:
  56.8 43.2 all-gather.2
  112.8 52.6 all-gather.4
  179.0 49.9 reduce-scatter.1
where the time goes:
time: 315 us; the launch traced here: 311 us
  waiting for transfers between devices  97.4 us (31%)
  starting transfers between devices  88.3 us (28%)
  matrix products  54.9 us (17%)
  other arithmetic  32.3 us (10%)
  local copies, waits for them, and re-layouts  17 us (5%)
  between operations  16.2 us (5%)
  Pallas kernels  4.56 us (1%)
    ppermute x35, waiting for transfers between devices, moved(): return lax.ppermute(rows, AXES, pairs)  93 us
    ppermute x35, starting transfers between devices, moved(): return lax.ppermute(rows, AXES, pairs)  64.5 us
    dot_general x19, matrix products, dot(): lax.dot_general(a, b, (((ca,), (cb,)), ((), ())), preferred_element_type=...  54.9 us
    unnamed x151, local copies, waits for them, and re-layouts  7.95 us
    ppermute x2, starting transfers between devices, extended(): lax.ppermute(tail, 'expert', [(i, i + 1) for i in range(ends)])  7.73 us
    all_to_all x1, starting transfers between devices, local(): taps = lax.all_to_all(taps, 'expert', 0, 0, tiled=True)  7.37 us
    reduce_sum x1, other arithmetic, rms_scale(): jnp.mean(values * values, axis=-1, keepdims=True) + EPSILON  6.32 us
  transfers between devices with their start and end apart: 44, of which 24 were waited for; matrix products, arithmetic and copies ran while one was open for 30% of the time, Pallas kernels for 0%

commit v1 on v0

--- a/solution.py
+++ b/solution.py
@@ -109,13 +109,15 @@
 
 def sent_back(first, other, second, arrange, grad_in, grad_out):
     part = 4 * SLOTS
-    same = total(
-        second[: 2 * part],
+    s1, s3, s2, up, down = together(
         moved(first[: 2 * part], dx=-1),
         moved(first[2 * part :], dx=1),
         moved(second[2 * part :], dx=2),
-    )
-    other = total(moved(other[: 2 * part], dz=-1), moved(other[2 * part :], dz=1))
+        moved(other[: 2 * part], dz=-1),
+        moved(other[2 * part :], dz=1),
+    )
+    same = total(second[: 2 * part], s1, s3, s2)
+    other = total(up, down)
     same, other, grad_in, grad_out = together(same, other, grad_in, grad_out)
     core = moved(jnp.concatenate([same[part:], other[part:]], axis=0), dc=1)
     placed = jnp.concatenate([same[:part], other[:part], core], axis=0)
@@ -295,6 +297,7 @@
     )
     pre_cots = jnp.concatenate([first_pre_cot, second_pre_cot], axis=0)
     normeds = jnp.concatenate([first_normed, second_normed], axis=0)
+    pre_cots, normeds, other_part = together(pre_cots, normeds, other_part)
     grad_in = grad_in + dot(normeds, pre_cots, 0, 0)
     returned, grad_in, grad_out = sent_back(
         first_sum, other_part, second_sum, arrange, grad_in, grad_out

time: 315 us -> 316 us (level)
  waiting for transfers between devices: 97.4 us -> 85.8 us
  matrix products: 54.9 us -> 60.3 us
  starting transfers between devices: 88.3 us -> 91.7 us
  other arithmetic: 32.3 us -> 35.6 us
    ppermute x35, waiting for transfers between devices: 93 us -> 81.5 us  [moved(): return lax.ppermute(rows, AXES, pairs)]
    dot_general x19, matrix products: 54.9 us -> 60.3 us  [dot(): lax.dot_general(a, b, (((ca,), (cb,)), ((), ())), preferred_element_type=...]
    concatenate x0 -> x2, other arithmetic: none -> 3.32 us  [the longest x1 1.98 us: local(): normeds = jnp.concatenate([first_normed, second_normed], axis=0)]
  transfers between devices with their start and end apart: 44 -> 44, of which waited for: 24 -> 20; matrix products, arithmetic and copies ran while one was open for 30% -> 32% of each run, Pallas kernels for 0% -> 0%
where the time goes in v1:
time: 316 us; the launch traced here: 312 us
  starting transfers between devices  91.7 us (29%)
  waiting for transfers between devices  85.8 us (27%)
  matrix products  60.3 us (19%)
  other arithmetic  35.6 us (11%)
  local copies, waits for them, and re-layouts  17.9 us (6%)
  between operations  16.1 us (5%)
  Pallas kernels  4.56 us (1%)
    ppermute x35, waiting for transfers between devices, moved(): return lax.ppermute(rows, AXES, pairs)  81.5 us
    ppermute x35, starting transfers between devices, moved(): return lax.ppermute(rows, AXES, pairs)  65.6 us
    dot_general x19, matrix products, dot(): lax.dot_general(a, b, (((ca,), (cb,)), ((), ())), preferred_element_type=...  60.3 us
    unnamed x151, local copies, waits for them, and re-layouts  7.96 us
    all_to_all x1, starting transfers between devices, local(): taps = lax.all_to_all(taps, 'expert', 0, 0, tiled=True)  7.95 us
    ppermute x2, starting transfers between devices, extended(): lax.ppermute(tail, 'expert', [(i, i + 1) for i in range(ends)])  7.73 us
  transfers between devices with their start and end apart: 44, of which 20 were waited for; matrix products, arithmetic and copies ran while one was open for 32% of the time, Pallas kernels for 0%

profile of v1, /device:TPU:1, one launch (start us, length us, event | category | flops | bytes accessed | tf_op | source)
XLA Modules:
  0.0 312.1 jit_solution(16474798965816646386)
XLA Ops:
  9.2 4.6 %collective-permute-start.3 = (bf16[15,1536]{1,0:T(8,128)(2,1)S(1)}, bf16[15,1536]{1,0:T(8,128)(2,1)S(1)}, u32[]{:S(2)}, u32[]{:S(2)}) collective-permute-start(bf16[15,1536]{1,0:T(8,128)(2,1)S(1)} %get-tuple-element.205), channel_id=1, source_target_pairs={{0,1},{1,2},{2,3},{3,4},{4,5},{5,6},{6,7},{7,8},{8,9},{9,10},{10,1... | collective-permute-start | bytes 138248 | tf_op jit(solution)/shard_map/ppermute | solution.py:40
  26.0 6.3 %multiply_reduce_fusion.1 = (f32[128]{0:T(128)S(1)}, f32[128,1536]{1,0:T(8,128)S(1)}) fusion(bf16[15,1536]{1,0:T(8,128)(2,1)} %copy-done.23, bf16[128,1536]{1,0:T(8,128)(2,1)S(1)} %fusion.143, f32[1536]{0:T(1024)S(1)} %get-tuple-element.165, f32[1536]{0:T(1024)S(1)} %get-tuple-element.166, f32[1536]{0:T(1024)S(1)} %get-tuple-element.137, ...), kind=kLoop, calls=%fused_computation.269 | loop fusion | flops 36568960 | bytes 1856000 | tf_op jit(solution)/shard_map/jvp()/reduce_sum | solution.py:49
  38.1 3.8 %collective-permute-start.7 = (bf16[144,1536]{1,0:T(8,128)(2,1)S(1)}, bf16[144,1536]{1,0:T(8,128)(2,1)S(1)}, u32[]{:S(2)}, u32[]{:S(2)}) collective-permute-start(bf16[144,1536]{1,0:T(8,128)(2,1)S(1)} %pad_maximum_fusion.10), channel_id=1, source_target_pairs={{0,72},{1,73},{8,0},{9,1},{64,8},{65,9},{72,64},{73,65},{2,74},{3,... | collective-permute-start | bytes 1327112 | tf_op jit(solution)/shard_map/ppermute | solution.py:30
  44.5 6.6 %collective-permute-done.7 = bf16[144,1536]{1,0:T(8,128)(2,1)S(1)} collective-permute-done((bf16[144,1536]{1,0:T(8,128)(2,1)S(1)}, bf16[144,1536]{1,0:T(8,128)(2,1)S(1)}, u32[]{:S(2)}, u32[]{:S(2)}) %collective-permute-start.7) | collective-permute-done | bytes 442400 | tf_op jit(solution)/shard_map/ppermute | solution.py:30
  51.1 3.2 %collective-permute-done.6 = bf16[144,1536]{1,0:T(8,128)(2,1)S(1)} collective-permute-done((bf16[144,1536]{1,0:T(8,128)(2,1)S(1)}, bf16[144,1536]{1,0:T(8,128)(2,1)S(1)}, u32[]{:S(2)}, u32[]{:S(2)}) %collective-permute-start.6) | collective-permute-done | bytes 442400 | tf_op jit(solution)/shard_map/ppermute | solution.py:30
  68.8 5.6 %collective-permute-done.12 = bf16[72,1536]{1,0:T(8,128)(2,1)S(1)} collective-permute-done((bf16[72,1536]{1,0:T(8,128)(2,1)S(1)}, bf16[72,1536]{1,0:T(8,128)(2,1)S(1)}, u32[]{:S(2)}, u32[]{:S(2)}) %collective-permute-start.12) | collective-permute-done | bytes 221216 | tf_op jit(solution)/shard_map/ppermute | solution.py:30
  74.4 5.5 %collective-permute-done.11 = bf16[288,1536]{1,0:T(8,128)(2,1)S(1)} collective-permute-done((bf16[288,1536]{1,0:T(8,128)(2,1)S(1)}, bf16[288,1536]{1,0:T(8,128)(2,1)S(1)}, u32[]{:S(2)}, u32[]{:S(2)}) %collective-permute-start.11) | collective-permute-done | bytes 884768 | tf_op jit(solution)/shard_map/ppermute | solution.py:30
  88.4 11.7 %collective-permute-start.16 = (bf16[144,1536]{1,0:T(8,128)(2,1)S(1)}, bf16[144,1536]{1,0:T(8,128)(2,1)S(1)}, u32[]{:S(2)}, u32[]{:S(2)}) collective-permute-start(bf16[144,1536]{1,0:T(8,128)(2,1)S(1)} %pad_maximum_fusion.12), channel_id=1, source_target_pairs={{0,8},{1,9},{8,64},{9,65},{64,72},{65,73},{72,0},{73,1},{2,10},{3,... | collective-permute-start | bytes 1327112 | tf_op jit(solution)/shard_map/ppermute | solution.py:30
  102.9 9.6 %collective-permute-done.16 = bf16[144,1536]{1,0:T(8,128)(2,1)S(1)} collective-permute-done((bf16[144,1536]{1,0:T(8,128)(2,1)S(1)}, bf16[144,1536]{1,0:T(8,128)(2,1)S(1)}, u32[]{:S(2)}, u32[]{:S(2)}) %collective-permute-start.16) | collective-permute-done | bytes 442400 | tf_op jit(solution)/shard_map/ppermute | solution.py:30
  118.2 9.9 %collective-permute-done.20 = bf16[144,1536]{1,0:T(8,128)(2,1)} collective-permute-done((bf16[144,1536]{1,0:T(8,128)(2,1)}, bf16[144,1536]{1,0:T(8,128)(2,1)}, u32[]{:S(2)}, u32[]{:S(2)}) %collective-permute-start.20) | collective-permute-done | bytes 442400 | tf_op jit(solution)/shard_map/ppermute | solution.py:30
  128.0 3.4 %collective-permute-done.19 = bf16[144,1536]{1,0:T(8,128)(2,1)} collective-permute-done((bf16[144,1536]{1,0:T(8,128)(2,1)}, bf16[144,1536]{1,0:T(8,128)(2,1)}, u32[]{:S(2)}, u32[]{:S(2)}) %collective-permute-start.19) | collective-permute-done | bytes 442400 | tf_op jit(solution)/shard_map/ppermute | solution.py:30
  131.4 3.8 %collective-permute-done.18 = bf16[288,1536]{1,0:T(8,128)(2,1)S(1)} collective-permute-done((bf16[288,1536]{1,0:T(8,128)(2,1)}, bf16[288,1536]{1,0:T(8,128)(2,1)S(1)}, u32[]{:S(2)}, u32[]{:S(2)}) %collective-permute-start.18) | collective-permute-done | bytes 884768 | tf_op jit(solution)/shard_map/ppermute | solution.py:30
  140.8 4.7 %fusion.17 = f32[576,768]{1,0:T(8,128)} fusion(bf16[1,768,1536]{2,1,0:T(8,128)(2,1)} %param.14, bf16[288,1536]{1,0:T(8,128)(2,1)S(1)} %collective-permute-done.18, bf16[288,1536]{1,0:T(8,128)(2,1)} %get-tuple-element.78), kind=kOutput, calls=%fused_computation.59 | convolution fusion | flops 1362493440 | bytes 5898240 | tf_op jit(solution)/shard_map/dot_general | solution.py:53
  145.5 7.5 %fusion.15 = f32[1152,768]{1,0:T(8,128)} fusion(bf16[1152,1536]{1,0:T(8,128)(2,1)} %all-gather.3.cloned.1.call-done, bf16[1,768,1536]{2,1,0:T(8,128)(2,1)} %param.14), kind=kOutput, calls=%fused_computation.57 | convolution fusion | flops 2717908992 | bytes 9437184 | tf_op jit(solution)/shard_map/dot_general | solution.py:53
  153.0 5.2 %collective-permute-done.21 = bf16[144,1536]{1,0:T(8,128)(2,1)} collective-permute-done((bf16[144,1536]{1,0:T(8,128)(2,1)}, bf16[144,1536]{1,0:T(8,128)(2,1)}, u32[]{:S(2)}, u32[]{:S(2)}) %collective-permute-start.21) | collective-permute-done | bytes 442400 | tf_op jit(solution)/shard_map/ppermute | solution.py:30
  166.4 5.1 %fusion.13 = f32[1152,768]{1,0:T(8,128)S(1)} fusion(bf16[1152,1536]{1,0:T(8,128)(2,1)} %all-gather.5.cloned.1.call-done, bf16[1,1536,768]{2,1,0:T(8,128)(2,1)S(1)} %copy-done), kind=kOutput, calls=%fused_computation.55 | convolution fusion | flops 2717908992 | bytes 9437184 | tf_op jit(solution)/shard_map/dot_general | solution.py:53
  175.3 4.5 %convolution_convert_fusion = bf16[1152,1536]{1,0:T(8,128)(2,1)} fusion(bf16[1152,768]{1,0:T(8,128)(2,1)S(1)} %get-tuple-element.109, bf16[1,1536,768]{2,1,0:T(8,128)(2,1)S(1)} %copy-done), kind=kOutput, calls=%fused_computation | convolution fusion | flops 2719678464 | bytes 7667712 | tf_op jit(solution)/shard_map/dot_general | solution.py:53
  179.8 4.0 %multiply_convert_fusion.3 = (bf16[576,768]{1,0:T(8,128)(2,1)S(1)}, bf16[576,768]{1,0:T(8,128)(2,1)S(1)}) fusion(f32[576,768]{1,0:T(8,128)} %fusion.19, bf16[576,1536]{1,0:T(8,128)(2,1)} %pad_maximum_fusion.1, bf16[1,1536,768]{2,1,0:T(8,128)(2,1)S(1)} %copy-done), kind=kOutput, calls=%fused_computation.101 | convolution fusion | flops 1363820544 | bytes 7667712 | tf_op jit(solution)/shard_map/dot_general | solution.py:53
  187.0 3.0 collective-permute-start.27
  195.6 5.0 %fusion.228 = f32[1536,768]{1,0:T(8,128)} fusion(bf16[1152,1536]{1,0:T(8,128)(2,1)S(1)} %copy-done.70, bf16[1152,768]{1,0:T(8,128)(2,1)S(1)} %copy-done.14), kind=kOutput, calls=%fused_computation.456 | convolution fusion | flops 2717908992 | bytes 10027008 | tf_op jit(solution)/shard_map/dot_general | solution.py:53
  200.6 3.3 %fusion.229 = f32[768,1536]{1,0:T(8,128)S(1)} fusion(bf16[1152,768]{1,0:T(8,128)(2,1)S(1)} %copy-done.12, bf16[1152,1536]{1,0:T(8,128)(2,1)S(1)} %copy-done.69), kind=kOutput, calls=%fused_computation.457 | convolution fusion | flops 2717908992 | bytes 10027008 | tf_op jit(solution)/shard_map/dot_general | solution.py:53
  203.9 5.6 %convolution_add_fusion = f32[768,1536]{1,0:T(8,128)} fusion(f32[768,1536]{1,0:T(8,128)S(1)} %fusion.229, bf16[288,1536]{1,0:T(8,128)(2,1)S(1)} %copy-done.73, bf16[288,1536]{1,0:T(8,128)(2,1)S(1)} %copy-done.18, bf16[576,1536]{1,0:T(8,128)(2,1)S(1)} %copy-done.26, bf16[576,768]{1,0:T(8,128)(2,1)S(1)} %get-tuple-element.114, ...), kind=kOutput, calls=%fused_computation.29 | convolution fusion | flops 2733244416 | bytes 14745600 | tf_op jit(solution)/shard_map/dot_general | solution.py:53
  210.8 3.6 %collective-permute-start.28 = (bf16[144,1536]{1,0:T(8,128)(2,1)}, bf16[144,1536]{1,0:T(8,128)(2,1)}, u32[]{:S(2)}, u32[]{:S(2)}) collective-permute-start(bf16[144,1536]{1,0:T(8,128)(2,1)} %get-tuple-element.182), channel_id=1, source_target_pairs={{0,48},{1,49},{8,56},{9,57},{64,112},{65,113},{72,120},{73,121},{2... | collective-permute-start | bytes 1327112 | tf_op jit(solution)/shard_map/ppermute | solution.py:30
  214.4 13.2 %collective-permute-done.26 = bf16[288,1536]{1,0:T(8,128)(2,1)S(1)} collective-permute-done((bf16[288,1536]{1,0:T(8,128)(2,1)S(1)}, bf16[288,1536]{1,0:T(8,128)(2,1)S(1)}, u32[]{:S(2)}, u32[]{:S(2)}) %collective-permute-start.26) | collective-permute-done | bytes 884768 | tf_op jit(solution)/shard_map/ppermute | solution.py:30
  239.8 8.9 %convolution_add_fusion.1 = f32[1536,768]{1,0:T(8,128)} fusion(f32[1536,768]{1,0:T(8,128)} %fusion.228, bf16[1152,1536]{1,0:T(8,128)(2,1)} %pad_maximum_fusion, bf16[1152,768]{1,0:T(8,128)(2,1)S(1)} %copy-done.8), kind=kOutput, calls=%fused_computation.30 | convolution fusion | flops 2719088640 | bytes 14745600 | tf_op jit(solution)/shard_map/dot_general | solution.py:53
  263.0 5.7 %collective-permute-done.35 = bf16[72,1536]{1,0:T(8,128)(2,1)S(1)} collective-permute-done((bf16[72,1536]{1,0:T(8,128)(2,1)S(1)}, bf16[72,1536]{1,0:T(8,128)(2,1)S(1)}, u32[]{:S(2)}, u32[]{:S(2)}) %collective-permute-start.35) | collective-permute-done | bytes 221216 | tf_op jit(solution)/shard_map/ppermute | solution.py:30
  271.1 3.7 %tap_sums.1 = f32[8,32,256]{2,1,0:T(8,128)S(1)} custom-call(f32[128,1536]{1,0:T(8,128)S(1)} %fusion.144.resid_cot, bf16[160,1536]{1,0:T(8,128)(2,1)S(1)} %maximum_maximum_fusion.rim), custom_call_target="tpu_custom_call" | custom-call | tf_op jit(solution)/shard_map/tap_sums/pallas_call | solution.py:156
  275.5 5.2 %all-to-all-start = ((f32[8,32,256]{2,1,0:T(8,128)}), f32[8,32,256]{2,1,0:T(8,128)S(1)}, u32[]{:S(2)}, u32[]{:S(2)}) async-start(f32[8,32,256]{2,1,0:T(8,128)} %copy-done.1), calls=%async_computation.1 | async-start | bytes 524288 | tf_op jit(solution)/shard_map/all_to_all | solution.py:309
  281.4 3.2 %collective-permute-start.37 = (f32[15,1536]{1,0:T(8,128)}, f32[15,1536]{1,0:T(8,128)S(1)}, u32[]{:S(2)}, u32[]{:S(2)}) collective-permute-start(f32[15,1536]{1,0:T(8,128)} %get-tuple-element.195), channel_id=1, source_target_pairs={{1,0},{2,1},{3,2},{4,3},{5,4},{6,5},{7,6},{8,7},{9,8},{10,9},{11,1... | collective-permute-start | bytes 276488 | tf_op jit(solution)/shard_map/ppermute | solution.py:42
  284.6 3.1 %collective-permute-start.38 = (f32[15,1536]{1,0:T(8,128)}, f32[15,1536]{1,0:T(8,128)}, u32[]{:S(2)}, u32[]{:S(2)}) collective-permute-start(f32[15,1536]{1,0:T(8,128)} %get-tuple-element.196), channel_id=1, source_target_pairs={{0,1},{1,2},{2,3},{3,4},{4,5},{5,6},{6,7},{7,8},{8,9},{9,10},{10,1... | collective-permute-start | bytes 276488 | tf_op jit(solution)/shard_map/ppermute | solution.py:40
  289.6 8.0 %all-to-all-start.1 = ((f32[16,32,128]{2,1,0:T(8,128)}), f32[16,32,128]{2,1,0:T(8,128)S(1)}, u32[]{:S(2)}, u32[]{:S(2)}) async-start(f32[16,32,128]{2,1,0:T(8,128)} %split_columns.1), calls=%async_computation.2 | async-start | bytes 524288 | tf_op jit(solution)/shard_map/all_to_all | solution.py:310
  297.6 6.2 %fusion.177 = bf16[1,128,1536]{2,1,0:T(8,128)(2,1)} fusion(f32[128,1536]{1,0:T(8,128)S(1)} %fusion.144.resid_cot, f32[15,1536]{1,0:T(8,128)} %collective-permute-done.38, f32[1536]{0:T(1024)} %copy-done.58, f32[1536]{0:T(1024)} %copy-done.59, f32[1536]{0:T(1024)S(1)} %get-tuple-element.137, f32[1536]{0:T(1024)S(1)} %copy-done.28, f32[1536]{0:T(1024)S(1)} %copy-done.30, ...), kind=kLoop, calls=%fused_computation.329 | loop fusion | flops 18481152 | bytes 1554944 | tf_op jit(solution)/shard_map/broadcast_in_dim | solution.py:318
  (293 shorter events, 113.4 us)
Async XLA Ops:
  7.2 138.3 %all-gather.3.cloned.1.call-start = ((), (), s32[]{:S(2)}) async-start(), calls=%async_computation.3 | async-start | bytes 4423680 | tf_op jit(solution)/shard_map/all_gather | solution.py:100
  9.2 16.1 %collective-permute-start.3 = (bf16[15,1536]{1,0:T(8,128)(2,1)S(1)}, bf16[15,1536]{1,0:T(8,128)(2,1)S(1)}, u32[]{:S(2)}, u32[]{:S(2)}) collective-permute-start(bf16[15,1536]{1,0:T(8,128)(2,1)S(1)} %get-tuple-element.205), channel_id=1, source_target_pairs={{0,1},{1,2},{2,3},{3,4},{4,5},{5,6},{6,7},{7,8},{8,9},{9,10},{10,1... | collective-permute-start | bytes 138248 | tf_op jit(solution)/shard_map/ppermute | solution.py:40
  18.2 15.7 %collective-permute-start.2 = (bf16[72,1536]{1,0:T(8,128)(2,1)S(1)}, bf16[72,1536]{1,0:T(8,128)(2,1)S(1)}, u32[]{:S(2)}, u32[]{:S(2)}) collective-permute-start(bf16[72,1536]{1,0:T(8,128)(2,1)S(1)} %get-tuple-element.191), channel_id=1, source_target_pairs={{0,6},{1,7},{8,14},{9,15},{64,70},{65,71},{72,78},{73,79},{2,0},{3... | collective-permute-start | bytes 663560 | tf_op jit(solution)/shard_map/ppermute | solution.py:30
  21.0 12.9 %collective-permute-start.1 = (bf16[72,1536]{1,0:T(8,128)(2,1)S(1)}, bf16[72,1536]{1,0:T(8,128)(2,1)S(1)}, u32[]{:S(2)}, u32[]{:S(2)}) collective-permute-start(bf16[72,1536]{1,0:T(8,128)(2,1)S(1)} %get-tuple-element.192), channel_id=1, source_target_pairs={{0,4},{1,5},{8,12},{9,13},{64,68},{65,69},{72,76},{73,77},{2,6},{3... | collective-permute-start | bytes 663560 | tf_op jit(solution)/shard_map/ppermute | solution.py:30
  21.3 13.2 %collective-permute-start = (bf16[72,1536]{1,0:T(8,128)(2,1)S(1)}, bf16[72,1536]{1,0:T(8,128)(2,1)S(1)}, u32[]{:S(2)}, u32[]{:S(2)}) collective-permute-start(bf16[72,1536]{1,0:T(8,128)(2,1)S(1)} %get-tuple-element.193), channel_id=1, source_target_pairs={{0,2},{1,3},{8,10},{9,11},{64,66},{65,67},{72,74},{73,75},{2,4},{3... | collective-permute-start | bytes 663560 | tf_op jit(solution)/shard_map/ppermute | solution.py:30
  38.1 13.0 %collective-permute-start.7 = (bf16[144,1536]{1,0:T(8,128)(2,1)S(1)}, bf16[144,1536]{1,0:T(8,128)(2,1)S(1)}, u32[]{:S(2)}, u32[]{:S(2)}) collective-permute-start(bf16[144,1536]{1,0:T(8,128)(2,1)S(1)} %pad_maximum_fusion.10), channel_id=1, source_target_pairs={{0,72},{1,73},{8,0},{9,1},{64,8},{65,9},{72,64},{73,65},{2,74},{3,... | collective-permute-start | bytes 1327112 | tf_op jit(solution)/shard_map/ppermute | solution.py:30
  41.9 12.4 %collective-permute-start.6 = (bf16[144,1536]{1,0:T(8,128)(2,1)S(1)}, bf16[144,1536]{1,0:T(8,128)(2,1)S(1)}, u32[]{:S(2)}, u32[]{:S(2)}) collective-permute-start(bf16[144,1536]{1,0:T(8,128)(2,1)S(1)} %pad_maximum_fusion.10), channel_id=1, source_target_pairs={{0,8},{1,9},{8,64},{9,65},{64,72},{65,73},{72,0},{73,1},{2,10},{3,... | collective-permute-start | bytes 1327112 | tf_op jit(solution)/shard_map/ppermute | solution.py:30
  41.9 12.3 %collective-permute-start.9 = (bf16[144,1536]{1,0:T(8,128)(2,1)S(1)}, bf16[144,1536]{1,0:T(8,128)(2,1)}, u32[]{:S(2)}, u32[]{:S(2)}) collective-permute-start(bf16[144,1536]{1,0:T(8,128)(2,1)S(1)} %pad_maximum_fusion.11), channel_id=1, source_target_pairs={{0,48},{1,49},{8,56},{9,57},{64,112},{65,113},{72,120},{73,121},{2... | collective-permute-start | bytes 1327112 | tf_op jit(solution)/shard_map/ppermute | solution.py:30
  44.5 12.1 %collective-permute-start.8 = (bf16[144,1536]{1,0:T(8,128)(2,1)S(1)}, bf16[144,1536]{1,0:T(8,128)(2,1)}, u32[]{:S(2)}, u32[]{:S(2)}) collective-permute-start(bf16[144,1536]{1,0:T(8,128)(2,1)S(1)} %pad_maximum_fusion.11), channel_id=1, source_target_pairs={{0,16},{1,17},{8,24},{9,25},{64,80},{65,81},{72,88},{73,89},{2,18}... | collective-permute-start | bytes 1327112 | tf_op jit(solution)/shard_map/ppermute | solution.py:30
  57.6 108.8 %all-gather.5.cloned.1.call-start = ((), (), s32[]{:S(2)}) async-start(), calls=%async_computation.4 | async-start | bytes 4423680 | tf_op jit(solution)/shard_map/all_gather | solution.py:100
  57.6 16.8 %collective-permute-start.10 = (bf16[144,1536]{1,0:T(8,128)(2,1)}, bf16[144,1536]{1,0:T(8,128)(2,1)S(1)}, u32[]{:S(2)}, u32[]{:S(2)}) collective-permute-start(bf16[144,1536]{1,0:T(8,128)(2,1)} %collective-permute-done.8), channel_id=1, source_target_pairs={{0,16},{1,17},{8,24},{9,25},{64,80},{65,81},{72,88},{73,89},{2,18}... | collective-permute-start | bytes 1327112 | tf_op jit(solution)/shard_map/ppermute | solution.py:30
  59.0 20.9 %collective-permute-start.11 = (bf16[288,1536]{1,0:T(8,128)(2,1)S(1)}, bf16[288,1536]{1,0:T(8,128)(2,1)S(1)}, u32[]{:S(2)}, u32[]{:S(2)}) collective-permute-start(bf16[288,1536]{1,0:T(8,128)(2,1)S(1)} %pad_maximum_fusion.4), channel_id=1, source_target_pairs={{0,64},{1,65},{8,72},{9,73},{64,0},{65,1},{72,8},{73,9},{2,66},{3,... | collective-permute-start | bytes 2654216 | tf_op jit(solution)/shard_map/ppermute | solution.py:30
  85.9 16.9 %collective-permute-start.17 = (bf16[144,1536]{1,0:T(8,128)(2,1)S(1)}, bf16[144,1536]{1,0:T(8,128)(2,1)S(1)}, u32[]{:S(2)}, u32[]{:S(2)}) collective-permute-start(bf16[144,1536]{1,0:T(8,128)(2,1)S(1)} %pad_maximum_fusion.12), channel_id=1, source_target_pairs={{0,72},{1,73},{8,0},{9,1},{64,8},{65,9},{72,64},{73,65},{2,74},{3,... | collective-permute-start | bytes 1327112 | tf_op jit(solution)/shard_map/ppermute | solution.py:30
  88.4 24.1 %collective-permute-start.16 = (bf16[144,1536]{1,0:T(8,128)(2,1)S(1)}, bf16[144,1536]{1,0:T(8,128)(2,1)S(1)}, u32[]{:S(2)}, u32[]{:S(2)}) collective-permute-start(bf16[144,1536]{1,0:T(8,128)(2,1)S(1)} %pad_maximum_fusion.12), channel_id=1, source_target_pairs={{0,8},{1,9},{8,64},{9,65},{64,72},{65,73},{72,0},{73,1},{2,10},{3,... | collective-permute-start | bytes 1327112 | tf_op jit(solution)/shard_map/ppermute | solution.py:30
  113.5 122.0 %reduce-scatter.2.cloned.1.call-start = ((), (), s32[]{:S(2)}) async-start(), calls=%async_computation.5 | async-start | bytes 4423680 | tf_op jit(solution)/shard_map/reduce_scatter | solution.py:292
  113.6 21.6 %collective-permute-start.18 = (bf16[288,1536]{1,0:T(8,128)(2,1)}, bf16[288,1536]{1,0:T(8,128)(2,1)S(1)}, u32[]{:S(2)}, u32[]{:S(2)}) collective-permute-start(bf16[288,1536]{1,0:T(8,128)(2,1)} %get-tuple-element.78), channel_id=1, source_target_pairs={{0,64},{1,65},{8,72},{9,73},{64,0},{65,1},{72,8},{73,9},{2,66},{3,... | collective-permute-start | bytes 2654216 | tf_op jit(solution)/shard_map/ppermute | solution.py:30
  115.6 12.5 %collective-permute-start.20 = (bf16[144,1536]{1,0:T(8,128)(2,1)}, bf16[144,1536]{1,0:T(8,128)(2,1)}, u32[]{:S(2)}, u32[]{:S(2)}) collective-permute-start(bf16[144,1536]{1,0:T(8,128)(2,1)} %pad_maximum_fusion.13), channel_id=1, source_target_pairs={{0,48},{1,49},{8,56},{9,57},{64,112},{65,113},{72,120},{73,121},{2... | collective-permute-start | bytes 1327112 | tf_op jit(solution)/shard_map/ppermute | solution.py:30
  118.2 13.3 %collective-permute-start.19 = (bf16[144,1536]{1,0:T(8,128)(2,1)}, bf16[144,1536]{1,0:T(8,128)(2,1)}, u32[]{:S(2)}, u32[]{:S(2)}) collective-permute-start(bf16[144,1536]{1,0:T(8,128)(2,1)} %pad_maximum_fusion.13), channel_id=1, source_target_pairs={{0,16},{1,17},{8,24},{9,25},{64,80},{65,81},{72,88},{73,89},{2,18}... | collective-permute-start | bytes 1327112 | tf_op jit(solution)/shard_map/ppermute | solution.py:30
  135.2 23.0 %collective-permute-start.23 = (bf16[144,1536]{1,0:T(8,128)(2,1)}, bf16[144,1536]{1,0:T(8,128)(2,1)}, u32[]{:S(2)}, u32[]{:S(2)}) collective-permute-start(bf16[144,1536]{1,0:T(8,128)(2,1)} %collective-permute-done.20), channel_id=1, source_target_pairs={{0,48},{1,49},{8,56},{9,57},{64,112},{65,113},{72,120},{73,121},{2... | collective-permute-start | bytes 1327112 | tf_op jit(solution)/shard_map/ppermute | solution.py:30
  137.8 20.4 %collective-permute-start.22 = (bf16[144,1536]{1,0:T(8,128)(2,1)}, bf16[144,1536]{1,0:T(8,128)(2,1)}, u32[]{:S(2)}, u32[]{:S(2)}) collective-permute-start(bf16[144,1536]{1,0:T(8,128)(2,1)} %collective-permute-done.20), channel_id=1, source_target_pairs={{0,64},{1,65},{8,72},{9,73},{64,0},{65,1},{72,8},{73,9},{2,66},{3,... | collective-permute-start | bytes 1327112 | tf_op jit(solution)/shard_map/ppermute | solution.py:30
  138.2 20.0 %collective-permute-start.21 = (bf16[144,1536]{1,0:T(8,128)(2,1)}, bf16[144,1536]{1,0:T(8,128)(2,1)}, u32[]{:S(2)}, u32[]{:S(2)}) collective-permute-start(bf16[144,1536]{1,0:T(8,128)(2,1)} %collective-permute-done.19), channel_id=1, source_target_pairs={{0,64},{1,65},{8,72},{9,73},{64,0},{65,1},{72,8},{73,9},{2,66},{3,... | collective-permute-start | bytes 1327112 | tf_op jit(solution)/shard_map/ppermute | solution.py:30
  158.2 21.6 %collective-permute-start.24 = (bf16[144,1536]{1,0:T(8,128)(2,1)}, bf16[144,1536]{1,0:T(8,128)(2,1)}, u32[]{:S(2)}, u32[]{:S(2)}) collective-permute-start(bf16[144,1536]{1,0:T(8,128)(2,1)} %pad_maximum_fusion.13), channel_id=1, source_target_pairs={{0,64},{1,65},{8,72},{9,73},{64,0},{65,1},{72,8},{73,9},{2,66},{3,... | collective-permute-start | bytes 1327112 | tf_op jit(solution)/shard_map/ppermute | solution.py:30
  158.2 21.6 %collective-permute-start.25 = (bf16[144,1536]{1,0:T(8,128)(2,1)}, bf16[144,1536]{1,0:T(8,128)(2,1)}, u32[]{:S(2)}, u32[]{:S(2)}) collective-permute-start(bf16[144,1536]{1,0:T(8,128)(2,1)} %collective-permute-done.23), channel_id=1, source_target_pairs={{0,64},{1,65},{8,72},{9,73},{64,0},{65,1},{72,8},{73,9},{2,66},{3,... | collective-permute-start | bytes 1327112 | tf_op jit(solution)/shard_map/ppermute | solution.py:30
  187.0 22.5 %collective-permute-start.27 = (bf16[288,1536]{1,0:T(8,128)(2,1)S(1)}, bf16[288,1536]{1,0:T(8,128)(2,1)S(1)}, u32[]{:S(2)}, u32[]{:S(2)}) collective-permute-start(bf16[288,1536]{1,0:T(8,128)(2,1)S(1)} %slice.705), channel_id=1, source_target_pairs={{0,64},{1,65},{8,72},{9,73},{64,0},{65,1},{72,8},{73,9},{2,66},{3,... | collective-permute-start | bytes 2654216 | tf_op jit(solution)/shard_map/ppermute | solution.py:30
  194.1 33.5 %collective-permute-start.26 = (bf16[288,1536]{1,0:T(8,128)(2,1)S(1)}, bf16[288,1536]{1,0:T(8,128)(2,1)S(1)}, u32[]{:S(2)}, u32[]{:S(2)}) collective-permute-start(bf16[288,1536]{1,0:T(8,128)(2,1)S(1)} %slice.702), channel_id=1, source_target_pairs={{0,64},{1,65},{8,72},{9,73},{64,0},{65,1},{72,8},{73,9},{2,66},{3,... | collective-permute-start | bytes 2654216 | tf_op jit(solution)/shard_map/ppermute | solution.py:30
  210.7 38.0 %collective-permute-start.29 = (bf16[144,1536]{1,0:T(8,128)(2,1)}, bf16[144,1536]{1,0:T(8,128)(2,1)}, u32[]{:S(2)}, u32[]{:S(2)}) collective-permute-start(bf16[144,1536]{1,0:T(8,128)(2,1)} %get-tuple-element.181), channel_id=1, source_target_pairs={{0,16},{1,17},{8,24},{9,25},{64,80},{65,81},{72,88},{73,89},{2,18}... | collective-permute-start | bytes 1327112 | tf_op jit(solution)/shard_map/ppermute | solution.py:30
  210.8 37.9 %collective-permute-start.28 = (bf16[144,1536]{1,0:T(8,128)(2,1)}, bf16[144,1536]{1,0:T(8,128)(2,1)}, u32[]{:S(2)}, u32[]{:S(2)}) collective-permute-start(bf16[144,1536]{1,0:T(8,128)(2,1)} %get-tuple-element.182), channel_id=1, source_target_pairs={{0,48},{1,49},{8,56},{9,57},{64,112},{65,113},{72,120},{73,121},{2... | collective-permute-start | bytes 1327112 | tf_op jit(solution)/shard_map/ppermute | solution.py:30
  229.5 19.2 %collective-permute-start.30 = (bf16[144,1536]{1,0:T(8,128)(2,1)}, bf16[144,1536]{1,0:T(8,128)(2,1)}, u32[]{:S(2)}, u32[]{:S(2)}) collective-permute-start(bf16[144,1536]{1,0:T(8,128)(2,1)} %slice.706), channel_id=1, source_target_pairs={{0,32},{1,33},{8,40},{9,41},{64,96},{65,97},{72,104},{73,105},{2,3... | collective-permute-start | bytes 1327112 | tf_op jit(solution)/shard_map/ppermute | solution.py:30
  275.5 13.1 %all-to-all-start = ((f32[8,32,256]{2,1,0:T(8,128)}), f32[8,32,256]{2,1,0:T(8,128)S(1)}, u32[]{:S(2)}, u32[]{:S(2)}) async-start(f32[8,32,256]{2,1,0:T(8,128)} %copy-done.1), calls=%async_computation.1 | async-start | bytes 524288 | tf_op jit(solution)/shard_map/all_to_all | solution.py:309
  281.4 16.2 %collective-permute-start.37 = (f32[15,1536]{1,0:T(8,128)}, f32[15,1536]{1,0:T(8,128)S(1)}, u32[]{:S(2)}, u32[]{:S(2)}) collective-permute-start(f32[15,1536]{1,0:T(8,128)} %get-tuple-element.195), channel_id=1, source_target_pairs={{1,0},{2,1},{3,2},{4,3},{5,4},{6,5},{7,6},{8,7},{9,8},{10,9},{11,1... | collective-permute-start | bytes 276488 | tf_op jit(solution)/shard_map/ppermute | solution.py:42
  284.6 13.0 %collective-permute-start.38 = (f32[15,1536]{1,0:T(8,128)}, f32[15,1536]{1,0:T(8,128)}, u32[]{:S(2)}, u32[]{:S(2)}) collective-permute-start(f32[15,1536]{1,0:T(8,128)} %get-tuple-element.196), channel_id=1, source_target_pairs={{0,1},{1,2},{2,3},{3,4},{4,5},{5,6},{6,7},{7,8},{8,9},{9,10},{10,1... | collective-permute-start | bytes 276488 | tf_op jit(solution)/shard_map/ppermute | solution.py:40
  289.6 15.1 %all-to-all-start.1 = ((f32[16,32,128]{2,1,0:T(8,128)}), f32[16,32,128]{2,1,0:T(8,128)S(1)}, u32[]{:S(2)}, u32[]{:S(2)}) async-start(f32[16,32,128]{2,1,0:T(8,128)} %split_columns.1), calls=%async_computation.2 | async-start | bytes 524288 | tf_op jit(solution)/shard_map/all_to_all | solution.py:310
  (86 other events, 1164.4 us)
Sparse Core Ops, SparseCore 0:
  57.7 43.2 all-gather.2
  113.7 52.6 all-gather.4
  179.9 49.9 reduce-scatter.1
